TPU v7x, 32 devices: a whole 2x2x4 slice. The times are simulated.
32 devices in a mesh: parts: 1, batch: 16 (over z, y, core), mp: 2 (over x).
Axes of the slice: x: 2, y: 2, z: 4, core: 2. Of those that a mesh axis runs over, the one named last changes fastest.
Arguments:
- activations: bfloat16 [4096, 4096], P(('parts', 'batch'), 'mp'), may hold values from -6 to 6
- output_gradient: bfloat16 [4096, 4096], P(('parts', 'batch'), 'mp'), may hold values from -6 to 6
- levels: bfloat16 [4096, 4096], P('mp', 'batch'), may hold values from -0.09375 to 0.09375
- scales: bfloat16 [4096, 64], P('mp', 'batch'), may hold values from 0.5 to 2
- adapter_down_rows: bfloat16 [512, 4096], P(('parts', 'batch'), 'mp'), may hold values from -0.09375 to 0.09375
- adapter_up_rows: bfloat16 [512, 4096], P(('parts', 'batch'), 'mp'), may hold values from -0.09375 to 0.09375
- tenant_per_tile: int32 [32, 1], P(('parts', 'batch')), may hold values from 0 to 31
- tenant_adapter_index: int32 [32], P('parts'), may hold values from 0 to 31, each once
Outputs:
- input_gradient: bfloat16 [4096, 4096], P(('parts', 'batch'), 'mp')
- down_grads: float32 [512, 4096], P(('parts', 'batch'), 'mp')
- up_grads: float32 [512, 4096], P(('parts', 'batch'), 'mp')
Inputs may be any that keep to these rules, and one draw needn't show every extreme that they name: `tenant_per_tile`: every tenant has some tile. `tenant_adapter_index`: each adapter serves exactly one tenant.
All inputs are finite; a program needn't handle non-finite values.
Results may differ from a plain program's by a relative error of at most 0.009.
Values may be sent and summed in bfloat16 or wider, within the bound.
A program may use at most 128 MiB of HBM per device.

v0:
```python
import jax
import jax.numpy as jnp
from jax import lax
from jax.sharding import PartitionSpec as P

ADAPTER_RANK = 16
QB = 64


def contract(left, right, left_dim, right_dim):
    return lax.dot_general(
        left, right, (((left_dim,), (right_dim,)), ((), ())), preferred_element_type=jnp.float32
    )


def dequantize(level_cols, scale_cols):
    return (
        level_cols.astype(jnp.float32) * jnp.repeat(scale_cols.astype(jnp.float32), QB, axis=1)
    ).astype(jnp.bfloat16)


def body(
    activations,
    output_gradient,
    levels,
    scales,
    adapter_down_rows,
    adapter_up_rows,
    tenant_per_tile,
    tenant_adapter_index,
):
    rows_dev, inner_local = activations.shape
    tiles_here = tenant_per_tile.shape[0]
    tile_rows = rows_dev // tiles_here
    adapter_count = tenant_adapter_index.shape[0]
    full_grads = lax.all_gather(output_gradient, "mp", axis=1, tiled=True)
    local_weight = dequantize(levels, scales)
    base_total = contract(
        full_grads, lax.all_gather(local_weight, "batch", axis=1, tiled=True), 1, 1
    )
    stacked_down_factors, all_up = (
        lax.all_gather(adapter_down_rows, "batch", axis=0, tiled=True),
        lax.all_gather(adapter_up_rows, "batch", axis=0, tiled=True),
    )
    tenants = tenant_per_tile[:, 0]
    adapter_ids = jnp.arange(adapter_count, dtype=jnp.int32)
    tenant_match = (tenants[:, None] == adapter_ids[None, :]).astype(jnp.int32)
    owner_of = jnp.sum(tenant_match * tenant_adapter_index[None, :], axis=1)
    tile_hot = owner_of[:, None] == adapter_ids[None, :]
    row_hot = jnp.broadcast_to(
        tile_hot[:, None, :], (tiles_here, tile_rows, adapter_count)
    ).reshape(rows_dev, adapter_count)
    onehot_float = row_hot.astype(jnp.float32)
    wide_hidden = contract(activations, stacked_down_factors, 1, 1).reshape(
        rows_dev, adapter_count, ADAPTER_RANK
    )
    wide_coeffs = contract(output_gradient, all_up, 1, 1).reshape(
        rows_dev, adapter_count, ADAPTER_RANK
    )
    hidden_share = jnp.sum(wide_hidden * onehot_float[:, :, None], axis=1)
    coefficient_share = jnp.sum(wide_coeffs * onehot_float[:, :, None], axis=1)
    adapter_hidden, adapter_coefficients = (
        lax.psum(hidden_share.astype(jnp.bfloat16), "mp").astype(jnp.float32),
        lax.psum(coefficient_share.astype(jnp.bfloat16), "mp").astype(jnp.float32),
    )
    hidden_narrow16 = adapter_hidden.astype(jnp.bfloat16)
    coefficients16 = adapter_coefficients.astype(jnp.bfloat16)
    hot16 = row_hot.astype(jnp.bfloat16)
    coefficients_widened = (hot16[:, :, None] * coefficients16[:, None, :]).reshape(
        rows_dev, adapter_count * ADAPTER_RANK
    )
    hidden_wide = (hot16[:, :, None] * hidden_narrow16[:, None, :]).reshape(
        rows_dev, adapter_count * ADAPTER_RANK
    )
    adapter_contribution = (
        2.0
        * jnp.dot(coefficients_widened, stacked_down_factors, preferred_element_type=jnp.float32)
    ).astype(jnp.bfloat16)
    down_terms = 2.0 * contract(coefficients_widened, activations, 0, 0)
    up_terms = 2.0 * contract(hidden_wide, output_gradient, 0, 0)
    down_grads, up_grads = (
        lax.psum_scatter(down_terms, "batch", scatter_dimension=0, tiled=True),
        lax.psum_scatter(up_terms, "batch", scatter_dimension=0, tiled=True),
    )
    input_gradient = (base_total + adapter_contribution.astype(jnp.float32)).astype(jnp.bfloat16)
    return (input_gradient, down_grads, up_grads)


def solution(mesh):
    in_specs = (
        P(("parts", "batch"), "mp"),
        P(("parts", "batch"), "mp"),
        P("mp", "batch"),
        P("mp", "batch"),
        P(("parts", "batch"), "mp"),
        P(("parts", "batch"), "mp"),
        P(("parts", "batch"), None),
        P("parts"),
    )
    out_specs = (
        P(("parts", "batch"), "mp"),
        P(("parts", "batch"), "mp"),
        P(("parts", "batch"), "mp"),
    )
    return jax.shard_map(body, mesh=mesh, in_specs=in_specs, out_specs=out_specs, check_vma=False)
```

profile of v0, /device:TPU:0, one launch (start us, length us, event | category | flops | bytes accessed | tf_op | source)
XLA Modules:
  0.0 417.9 jit_solution(16400416426750674144)
XLA Ops:
  7.2 0.7 all-gather.9.cloned.1.call-update
  8.0 0.7 all-gather.11.cloned.1.call-update
  8.7 0.7 all-gather.7.cloned.1.call-update
  9.5 1.5 copy.19
  11.0 1.2 fusion.4
  12.2 0.0 reduce-scatter.3.cloned.1.call-start
  12.3 0.2 fusion.7
  12.5 0.1 broadcast_in_dim.8
  12.6 0.1 broadcast_in_dim.7
  12.7 41.6 %all-gather.9.cloned.1.call-done = bf16[512,2048]{1,0:T(8,128)(2,1)} async-done(((bf16[32,2048]{1,0:T(8,128)(2,1)}), bf16[512,2048]{1,0:T(8,128)(2,1)}) %all-gather.9.cloned.1.call-update) | async-done | bytes 2097168 | tf_op jit(solution)/shard_map/all_gather | solution.py:43
  54.3 2.3 fusion.8
  56.7 40.0 %all-gather.11.cloned.1.call-done = bf16[512,2048]{1,0:T(8,128)(2,1)} async-done(((bf16[32,2048]{1,0:T(8,128)(2,1)}), bf16[512,2048]{1,0:T(8,128)(2,1)}) %all-gather.11.cloned.1.call-update) | async-done | bytes 2097168 | tf_op jit(solution)/shard_map/all_gather | solution.py:42
  96.7 2.3 fusion.9
  99.0 0.1 multiply_reduce_fusion
  99.2 8.1 %all-reduce = (bf16[256,16]{0,1:T(8,128)(2,1)S(1)}, bf16[256,16]{0,1:T(8,128)(2,1)S(1)}) all-reduce(bf16[256,16]{0,1:T(8,128)(2,1)S(1)} %get-tuple-element.13, bf16[256,16]{0,1:T(8,128)(2,1)S(1)} %get-tuple-element.12), channel_id=1, replica_groups=mesh['parts'=1,'batch'=16,'mp'=2] {'mp'}, use_global_device_ids=true, to_apply=%region_2.0 | all-reduce | flops 8192 | bytes 32768 | tf_op jit(solution)/shard_map/psum | solution.py:64
  107.3 2.7 convolution_multiply_fusion.1
  110.0 2.7 convolution_multiply_fusion
  112.7 3.9 fusion.3
  116.6 13.6 %all-gather.7.cloned.1.call-done = bf16[256,4096]{1,0:T(8,128)(2,1)} async-done(((bf16[256,2048]{1,0:T(8,128)(2,1)}), bf16[256,4096]{1,0:T(8,128)(2,1)}) %all-gather.7.cloned.1.call-update) | async-done | bytes 2097168 | tf_op jit(solution)/shard_map/all_gather | solution.py:36
  130.1 129.5 %all-gather.5.cloned.1.call-done = bf16[2048,4096]{0,1:T(8,128)(2,1)} async-done(((bf16[2048,256]{0,1:T(8,128)(2,1)}), bf16[2048,4096]{0,1:T(8,128)(2,1)}) %all-gather.5.cloned.1.call-update) | async-done | bytes 16777232 | tf_op jit(solution)/shard_map/all_gather | solution.py:39
  259.7 12.0 %fusion.1 = bf16[256,2048]{0,1:T(8,128)(2,1)S(1)} fusion(f32[256,2048]{0,1:T(8,128)} %fusion.3, bf16[2048,4096]{0,1:T(8,128)(2,1)} %all-gather.5.cloned.1.call-done, bf16[256,4096]{1,0:T(8,128)(2,1)} %all-gather.7.cloned.1.call-done), kind=kOutput, calls=%fused_computation.5 | convolution fusion | flops 4296015872 | bytes 22020096 | tf_op jit(solution)/shard_map/dot_general | solution.py:11
  271.7 1.4 copy.23
  273.1 61.7 %reduce-scatter.3.cloned.1.call-done = f32[32,2048]{1,0:T(8,128)} async-done(((f32[512,2048]{1,0:T(8,128)}), f32[32,2048]{1,0:T(8,128)}) %reduce-scatter.3.cloned.1.call-update) | async-done | bytes 262160 | tf_op jit(solution)/shard_map/reduce_scatter | solution.py:82
  334.8 76.3 %reduce-scatter.5.cloned.1.call-done = f32[32,2048]{1,0:T(8,128)} async-done(((f32[512,2048]{1,0:T(8,128)}), f32[32,2048]{1,0:T(8,128)}) %reduce-scatter.5.cloned.1.call-update) | async-done | bytes 262160 | tf_op jit(solution)/shard_map/reduce_scatter | solution.py:83
  (23 shorter events, 0.3 us)
Async XLA Ops:
  7.2 89.5 %copy-start = (bf16[256,2048]{1,0:T(8,128)(2,1)S(1)}, bf16[256,2048]{1,0:T(8,128)(2,1)}, u32[]{:S(2)}) copy-start(bf16[256,2048]{1,0:T(8,128)(2,1)} %param.8) | copy-start | bytes 3145732
  7.2 3.8 copy-start.2
  7.2 47.1 %all-gather.9.cloned.1.call-start = ((), (), s32[]{:S(2)}) async-start(), calls=%async_computation.4 | async-start | bytes 2228224 | tf_op jit(solution)/shard_map/all_gather | solution.py:43
  7.9 88.8 %all-gather.11.cloned.1.call-start = ((), (), s32[]{:S(2)}) async-start(), calls=%async_computation.5 | async-start | bytes 2228224 | tf_op jit(solution)/shard_map/all_gather | solution.py:42
  8.7 121.5 %all-gather.7.cloned.1.call-start = ((), (), s32[]{:S(2)}) async-start(), calls=%async_computation.3 | async-start | bytes 3145728 | tf_op jit(solution)/shard_map/all_gather | solution.py:36
  9.4 250.3 %all-gather.5.cloned.1.call-start = ((), (), s32[]{:S(2)}) async-start(), calls=%async_computation.2 | async-start | bytes 17825792 | tf_op jit(solution)/shard_map/all_gather | solution.py:39
  11.0 1.3 copy-start.3
  11.0 1.3 copy-start.4
  11.0 43.3 %copy-start.1 = (bf16[256,2048]{1,0:T(8,128)(2,1)S(1)}, bf16[256,2048]{1,0:T(8,128)(2,1)}, u32[]{:S(2)}) copy-start(bf16[256,2048]{1,0:T(8,128)(2,1)} %param.9) | copy-start | bytes 3145732
  12.2 322.6 %reduce-scatter.3.cloned.1.call-start = ((), (), s32[]{:S(2)}) async-start(), calls=%async_computation.6 | async-start | bytes 4456448 | tf_op jit(solution)/shard_map/reduce_scatter | solution.py:82
  109.9 301.1 %reduce-scatter.5.cloned.1.call-start = ((), (), s32[]{:S(2)}) async-start(), calls=%async_computation.7 | async-start | bytes 4456448 | tf_op jit(solution)/shard_map/reduce_scatter | solution.py:83
Sparse Core Ops, SparseCore 0:
  10.2 44.0 all-gather.8
  56.5 40.1 all-gather.10
  98.2 31.8 all-gather.6
  132.7 126.8 all-gather.4
  263.9 70.8 reduce-scatter.2
  339.6 71.4 reduce-scatter.4
where the time goes:
time: 418 us
  waiting for transfers between devices  365 us (87%)
  matrix products  25.9 us (6%)
  between operations  14.2 us (3%)
  blocking collectives  8.06 us (2%)
    all_gather x1, waiting for transfers between devices, body(): lax.all_gather(local_weight, 'batch', axis=1, tiled=True)  130 us
    reduce_scatter x1, waiting for transfers between devices, body(): lax.psum_scatter(up_terms, 'batch', scatter_dimension=0, tiled=True)  76.3 us
    reduce_scatter x1, waiting for transfers between devices, body(): lax.psum_scatter(down_terms, 'batch', scatter_dimension=0, tiled=True)  61.7 us
    all_gather x1, waiting for transfers between devices, body(): lax.all_gather(adapter_up_rows, 'batch', axis=0, tiled=True)  41.6 us
    all_gather x1, waiting for transfers between devices, body(): lax.all_gather(adapter_down_rows, 'batch', axis=0, tiled=True)  40 us
    dot_general x5, matrix products, contract(): lax.dot_general(left, right, (((left_dim,), (right_dim,)), ((), ())), pre...  22 us
    all_gather x1, waiting for transfers between devices, body(): full_grads = lax.all_gather(output_gradient, 'mp', axis=1, tiled=True)  13.6 us
  transfers between devices with their start and end apart: 6, of which 6 were waited for; matrix products, arithmetic and copies ran while one was open for 7% of the time, Pallas kernels for 0%

commit v1 on v0

--- a/solution.py
+++ b/solution.py
@@ -1,6 +1,8 @@
 import jax
 import jax.numpy as jnp
 from jax import lax
+from jax.experimental import pallas as pl
+from jax.experimental.pallas import tpu as pltpu
 from jax.sharding import PartitionSpec as P
 
 ADAPTER_RANK = 16
@@ -85,6 +87,299 @@
     input_gradient = (base_total + adapter_contribution.astype(jnp.float32)).astype(jnp.bfloat16)
     return (input_gradient, down_grads, up_grads)
 
+DEPTH, PIECES, UP, DOWN, ACROSS, SIBLING = 4, 2, 0, 1, 2, 3
+CHUNK = 256
+
+
+def fused_kernel(
+    spots, act, grad, weight, down_own, up_own,
+    out, terms,
+    wbuf, fac, gfull, acc, share, theirs,
+    w_recv, w_send, f_recv, f_send, t_recv, t_send, x_recv, x_send,
+):
+    slots, pieces, piece_rows, width = wbuf.shape
+    tiles = spots.shape[0]
+    me, half = lax.axis_index("batch"), lax.axis_index("mp")
+    z, y, core = me // 4, (me // 2) % 2, me % 2
+    place = {
+        UP: {"batch": me + 4},
+        DOWN: {"batch": me - 4},
+        ACROSS: {"batch": z * 4 + (1 - y) * 2 + core},
+        SIBLING: {"batch": z * 4 + y * 2 + 1 - core},
+    }
+    partner = {"mp": 1 - half}
+    not_top, not_bottom = z < DEPTH - 1, z > 0
+
+    inner, upper = z * (3 - z) // 2, z // 2
+
+    def near(k):
+        v = inner + k - 2 * inner * k if k < 2 else k
+        return v + upper * (3 - 2 * v)
+
+    def slot(k, plane, column):
+        yy = y if plane == 0 else 1 - y
+        cc = core if column == 0 else 1 - core
+        return near(k) * 4 + yy * 2 + cc
+
+    barrier = pltpu.get_barrier_semaphore()
+    for way, there in ((UP, not_top), (DOWN, not_bottom)):
+        @pl.when(there)
+        def _(way=way):
+            pl.semaphore_signal(barrier, inc=1, device_id=place[way], device_id_type=pl.DeviceIdType.MESH)
+    for to in (place[ACROSS], place[SIBLING], partner):
+        pl.semaphore_signal(barrier, inc=1, device_id=to, device_id_type=pl.DeviceIdType.MESH)
+    pl.semaphore_wait(barrier, 4 + inner)
+
+    started = []
+
+    def copy(src, dst, send, recv, to):
+        return pltpu.make_async_remote_copy(
+            src_ref=src, dst_ref=dst, send_sem=send, recv_sem=recv,
+            device_id=to, device_id_type=pl.DeviceIdType.MESH,
+        )
+
+    def push(src, dst, send, recv, way, when=None):
+        moved = copy(src, dst, send.at[way], recv, place[way])
+        started.append((moved, when))
+        if when is None:
+            moved.start()
+        else:
+            pl.when(when)(moved.start)
+
+    def spread(src, dst, send, recv, k, across):
+        from_z = near(k)
+        push(src, dst, send, recv, UP, jnp.logical_and(from_z <= z, not_top))
+        push(src, dst, send, recv, DOWN, jnp.logical_and(from_z >= z, not_bottom))
+        if across:
+            push(src, dst, send, recv, ACROSS)
+        push(src, dst, send, recv, SIBLING)
+
+    def landed(ref, recv):
+        copy(ref, ref, x_send.at[0], recv, partner).wait_recv()
+
+    def weight_on(k, plane):
+        s = slot(k, plane, 0)
+        for p in range(pieces):
+            dst = wbuf.at[s, p]
+            src = weight.at[p] if k == 0 and plane == 0 else dst
+            if src is dst:
+                landed(dst, w_recv.at[s, p])
+            if plane == 0:
+                spread(src, dst, w_send.at[k, p], w_recv.at[s, p], k, True)
+            else:
+                push(src, dst, w_send.at[DEPTH + k, p], w_recv.at[s, p], SIBLING)
+
+    def weight_in(k, plane):
+        s = slot(k, plane, 1)
+        for p in range(pieces):
+            landed(wbuf.at[s, p], w_recv.at[s, p])
+
+    def multiply(k, plane, column):
+        s = slot(k, plane, column)
+        per_half = gfull.shape[2] // width
+        cols = pl.ds(pl.multiple_of((s % per_half) * width, width), width)
+        own = k == 0 and plane == 0 and column == 0
+        per_piece = piece_rows // CHUNK
+
+        @pl.loop(0, pieces * per_piece)
+        def _(j):
+            rows = pl.ds(pl.multiple_of((j % per_piece) * CHUNK, CHUNK), CHUNK)
+            block = weight[j // per_piece, rows, :] if own else wbuf[s, j // per_piece, rows, :]
+            acc[j] += contract(gfull[s // per_half, :, cols], block, 1, 1)
+
+    def factor_on(k, plane):
+        s = slot(k, plane, 0)
+        if k or plane:
+            landed(fac.at[s], f_recv.at[s])
+        spread(fac.at[s], fac.at[s], f_send.at[plane * DEPTH + k], f_recv.at[s], k, k == 0 and plane == 0)
+
+    def terms_on(k, plane):
+        s = slot(k, plane, 0)
+        if k or plane:
+            landed(terms.at[s], t_recv.at[s])
+        if plane == 0:
+            spread(terms.at[s], terms.at[s], t_send.at[k], t_recv.at[s], k, True)
+        else:
+            push(terms.at[s], terms.at[s], t_send.at[DEPTH + k], t_recv.at[s], SIBLING)
+
+    rank = down_own.shape[1]
+    for sub in range(down_own.shape[0]):
+        fac[me, 0, sub] = down_own[sub]
+        fac[me, 1, sub] = up_own[sub]
+    factor_on(0, 0)
+    weight_on(0, 0)
+    cross = copy(grad, gfull.at[half], x_send.at[0], x_recv.at[0], partner)
+    cross.start()
+    gfull[half] = grad[...]
+    share[...] = jnp.zeros_like(share)
+
+    factor_on(0, 1)
+    for k in range(1, DEPTH):
+        factor_on(k, 0)
+        factor_on(k, 1)
+    weight_on(1, 0)
+    for k in range(DEPTH):
+        for plane in range(2):
+            s = slot(k, plane, 1)
+            landed(fac.at[s], f_recv.at[s])
+
+    tile_rows = act.shape[0] // tiles
+    for t in range(tiles):
+        rows = pl.ds(t * tile_rows, tile_rows)
+        where, sub = spots[t, 0], spots[t, 1]
+        share[0, rows, :rank] = contract(act[rows, :], fac[where, 0, sub], 1, 1)
+        share[1, rows, :rank] = contract(grad[rows, :], fac[where, 1, sub], 1, 1)
+    swap = copy(share, theirs, x_send.at[1], x_recv.at[1], partner)
+    swap.start()
+    weight_on(2, 0)
+    landed(theirs, x_recv.at[1])
+    for t in range(tiles):
+        rows = pl.ds(t * tile_rows, tile_rows)
+        where, sub = spots[t, 0], spots[t, 1]
+        hidden = share[0, rows, :] + theirs[0, rows, :]
+        coeffs = share[1, rows, :] + theirs[1, rows, :]
+        factor = fac[where, 0, sub]
+        coeffs16 = coeffs[:, :rank].astype(jnp.bfloat16)
+        lora = (2.0 * contract(coeffs16, factor, 1, 0)).astype(jnp.bfloat16).astype(jnp.float32)
+        for j in range(acc.shape[0]):
+            acc[j, rows, :] = lora[:, j * CHUNK : (j + 1) * CHUNK]
+        turned = jnp.transpose(coeffs)[:rank].astype(jnp.bfloat16)
+        terms[me, 0, t] = (2.0 * contract(turned, act[rows, :], 1, 0)).astype(jnp.bfloat16)
+        turned = jnp.transpose(hidden)[:rank].astype(jnp.bfloat16)
+        terms[me, 1, t] = (2.0 * contract(turned, grad[rows, :], 1, 0)).astype(jnp.bfloat16)
+    terms_on(0, 0)
+
+    landed(gfull.at[1 - half], x_recv.at[0])
+    multiply(0, 0, 0)
+    multiply(1, 0, 0)
+    multiply(2, 0, 0)
+    weight_on(0, 1)
+    weight_on(1, 1)
+    weight_on(3, 0)
+    terms_on(1, 0)
+    multiply(3, 0, 0)
+    weight_in(0, 0)
+    multiply(0, 0, 1)
+    multiply(0, 1, 0)
+    multiply(1, 1, 0)
+    weight_in(1, 0)
+    multiply(1, 0, 1)
+    weight_on(2, 1)
+    terms_on(2, 0)
+    multiply(2, 1, 0)
+    weight_in(0, 1)
+    multiply(0, 1, 1)
+    weight_in(1, 1)
+    multiply(1, 1, 1)
+    weight_in(2, 0)
+    multiply(2, 0, 1)
+    terms_on(3, 0)
+    terms_on(0, 1)
+    terms_on(1, 1)
+    weight_in(3, 0)
+    multiply(3, 0, 1)
+    weight_in(2, 1)
+    multiply(2, 1, 1)
+    weight_on(3, 1)
+    terms_on(2, 1)
+    multiply(3, 1, 0)
+    terms_on(3, 1)
+    weight_in(3, 1)
+    multiply(3, 1, 1)
+    for j in range(acc.shape[0]):
+        out[:, j * CHUNK : (j + 1) * CHUNK] = acc[j].astype(jnp.bfloat16)
+    for k in range(DEPTH):
+        for plane in range(2):
+            s = slot(k, plane, 1)
+            landed(terms.at[s], t_recv.at[s])
+    cross.wait_send()
+    swap.wait_send()
+    for moved, when in started:
+        if when is None:
+            moved.wait_send()
+        else:
+            pl.when(when)(moved.wait_send)
+
+
+def fused_body(
+    activations,
+    output_gradient,
+    levels,
+    scales,
+    adapter_down_rows,
+    adapter_up_rows,
+    tenant_per_tile,
+    tenant_adapter_index,
+):
+    rows_dev, inner_local = activations.shape
+    in_rows, out_cols = levels.shape
+    tiles_here = tenant_per_tile.shape[0]
+    held = adapter_down_rows.shape[0] // ADAPTER_RANK
+    slots = lax.axis_size("batch")
+    adapter_ids = jnp.arange(tenant_adapter_index.shape[0], dtype=jnp.int32)
+
+    def owners(tenants):
+        match = (tenants[:, None] == adapter_ids[None, :]).astype(jnp.int32)
+        return jnp.sum(match * tenant_adapter_index[None, :], axis=1)
+
+    mine = owners(tenant_per_tile[:, 0])
+    spots = jnp.stack([mine // held, mine % held], axis=1)
+    everyone = lax.all_gather(tenant_per_tile, "batch", axis=0, tiled=True)
+    weight = dequantize(levels, scales).reshape(PIECES, in_rows // PIECES, out_cols)
+    factor_shape = (held, ADAPTER_RANK, inner_local)
+    vmem = pl.BlockSpec(memory_space=pltpu.VMEM)
+    dma = pltpu.SemaphoreType.DMA
+    bf16, f32 = jnp.bfloat16, jnp.float32
+    out, terms = pl.pallas_call(
+        fused_kernel,
+        out_shape=(
+            jax.ShapeDtypeStruct((rows_dev, in_rows), bf16),
+            jax.ShapeDtypeStruct((slots, 2, tiles_here, ADAPTER_RANK, inner_local), bf16),
+        ),
+        in_specs=[pl.BlockSpec(memory_space=pltpu.SMEM)] + [vmem] * 5,
+        out_specs=(vmem, vmem),
+        scratch_shapes=[
+            pltpu.VMEM((slots,) + weight.shape, bf16),
+            pltpu.VMEM((slots, 2) + factor_shape, bf16),
+            pltpu.VMEM((2, rows_dev, inner_local), bf16),
+            pltpu.VMEM((in_rows // CHUNK, rows_dev, CHUNK), f32),
+            pltpu.VMEM((2, rows_dev, 128), f32),
+            pltpu.VMEM((2, rows_dev, 128), f32),
+            dma((slots, PIECES)),
+            dma((2 * DEPTH, PIECES, 4)),
+            dma((slots,)),
+            dma((2 * DEPTH, 4)),
+            dma((slots,)),
+            dma((2 * DEPTH, 4)),
+            dma((2,)),
+            dma((2,)),
+        ],
+        compiler_params=pltpu.CompilerParams(
+            collective_id=0, has_side_effects=True, vmem_limit_bytes=52 * 2**20
+        ),
+        cost_estimate=pl.CostEstimate(
+            flops=2 * rows_dev * in_rows * out_cols * slots,
+            bytes_accessed=2**27,
+            transcendentals=0,
+        ),
+    )(
+        spots,
+        activations,
+        output_gradient,
+        weight,
+        adapter_down_rows.reshape(factor_shape),
+        adapter_up_rows.reshape(factor_shape),
+    )
+    row_of = jnp.repeat(owners(everyone[:, 0]), ADAPTER_RANK) * ADAPTER_RANK + jnp.tile(
+        jnp.arange(ADAPTER_RANK, dtype=jnp.int32), everyone.shape[0]
+    )
+    first = lax.axis_index("batch") * held * ADAPTER_RANK
+    own_rows = first + jnp.arange(held * ADAPTER_RANK, dtype=jnp.int32)
+    pick = (own_rows[:, None] == row_of[None, :]).astype(bf16)
+    down_grads = contract(pick, terms[:, 0].reshape(-1, inner_local), 1, 0)
+    up_grads = contract(pick, terms[:, 1].reshape(-1, inner_local), 1, 0)
+    return out, down_grads, up_grads
+
 
 def solution(mesh):
     in_specs = (
@@ -102,4 +397,6 @@
         P(("parts", "batch"), "mp"),
         P(("parts", "batch"), "mp"),
     )
-    return jax.shard_map(body, mesh=mesh, in_specs=in_specs, out_specs=out_specs, check_vma=False)
+    fused = mesh.shape["batch"] == 16 and mesh.shape["mp"] == 2 and mesh.shape["parts"] == 1
+    chosen = fused_body if fused else body
+    return jax.shard_map(chosen, mesh=mesh, in_specs=in_specs, out_specs=out_specs, check_vma=False)

time: 418 us -> 187 us (0.45)
  waiting for transfers between devices: 365 us -> 0 us
  Pallas kernels: 0 us -> 160 us
  matrix products: 25.9 us -> 3.99 us
  between operations: 14.2 us -> 1.4 us
  local copies, waits for them, and re-layouts: 3.14 us -> 8.68 us
    all_gather x4 -> x0, waiting for transfers between devices: 225 us -> none  [the longest x1 130 us: body(): lax.all_gather(local_weight, 'batch', axis=1, tiled=True)]
    pallas_call x0 -> x1, Pallas kernels: none -> 160 us  [fused_body(): pl.pallas_call(fused_kernel, out_shape=(jax.ShapeDtypeStruct((rows_dev, i...]
    reduce_scatter x2 -> x0, waiting for transfers between devices: 138 us -> none  [the longest x1 76.3 us: body(): lax.psum_scatter(up_terms, 'batch', scatter_dimension=0, tiled=True)]
    dot_general x5 -> x2, matrix products: 22 us -> 3.99 us  [contract(): lax.dot_general(left, right, (((left_dim,), (right_dim,)), ((), ())), pre...]
    unnamed x0 -> x1, blocking collectives: none -> 11.6 us
    psum x1 -> x0, blocking collectives: 8.06 us -> none  [body(): lax.psum(coefficient_share.astype(jnp.bfloat16), 'mp').astype(jnp.float32)]
  transfers between devices with their start and end apart: 6 -> 0, of which waited for: 6 -> 0; matrix products, arithmetic and copies ran while one was open for 7% -> 0% of each run, Pallas kernels for 0% -> 0%
where the time goes in v1:
time: 187 us
  Pallas kernels  160 us (86%)
  blocking collectives  11.6 us (6%)
  local copies, waits for them, and re-layouts  8.68 us (5%)
  matrix products  3.99 us (2%)
    pallas_call x1, Pallas kernels, fused_body(): pl.pallas_call(fused_kernel, out_shape=(jax.ShapeDtypeStruct((rows_dev, i...  160 us
    unnamed x1, blocking collectives  11.6 us
    slice x1, local copies, waits for them, and re-layouts, fused_body(): up_grads = contract(pick, terms[:, 1].reshape(-1, inner_local), 1, 0)  4.02 us
    dot_general x2, matrix products, contract(): lax.dot_general(left, right, (((left_dim,), (right_dim,)), ((), ())), pre...  3.99 us

profile of v1, /device:TPU:0, one launch (start us, length us, event | category | flops | bytes accessed | tf_op | source)
XLA Modules:
  0.0 186.8 jit_solution(16149602936319948009)
XLA Ops:
  0.6 0.0 copy-start.2
  0.6 0.9 fusion.9
  1.5 0.1 copy.22
  1.6 0.1 pad_add_fusion.spots
  1.7 1.5 copy.26
  3.2 0.0 copy-start
  3.2 0.0 copy-start.1
  3.2 0.2 fusion
  3.5 1.3 copy.27
  4.8 159.8 %shard_map.103 = (bf16[256,2048]{1,0:T(8,128)(2,1)S(1)}, bf16[16,2,2,16,2048]{4,3,2,1,0:T(8,128)(2,1)}) custom-call(s32[2,2]{1,0:T(2,128)S(1)} %pad_add_fusion.spots, bf16[256,2048]{1,0:T(8,128)(2,1)} %act.1, bf16[256,2048]{1,0:T(8,128)(2,1)} %grad.1, bf16[2,1024,256]{2,1,0:T(8,128)(2,1)} %bitcast.19, bf16[2,16,2048]{2,1,0:T(8,128)(2,1)S(1)} %bitcast.15, ...), custom_call_target="tpu_custom_call" | custom-call | flops 4294967296 | bytes 134217728 | tf_op jit(solution)/shard_map/pallas_call | solution.py:333
  164.6 0.0 copy-start.5
  164.6 0.0 copy-start.3
  164.6 0.0 copy-start.4
  164.6 4.0 %fusion.10 = (bf16[16,1,2,16,2048]{4,3,2,1,0:T(8,128)(2,1)S(1)}, bf16[16,1,2,16,2048]{4,3,2,1,0:T(8,128)(2,1)}) fusion(bf16[16,2,2,16,2048]{4,3,2,1,0:T(8,128)(2,1)} %get-tuple-element.6), kind=kLoop, calls=%fused_computation.26 | loop fusion | bytes 8388608 | tf_op jit(solution)/shard_map/slice | solution.py:380
  168.6 0.0 copy-done.5
  168.6 0.6 dynamic-slice
  169.9 0.1 bitcast_dynamic-update-slice_fusion
  170.0 11.6 %all-reduce = s32[32]{0:T(128)S(1)} all-reduce(s32[32]{0:T(128)S(1)} %bitcast_dynamic-update-slice_fusion), channel_id=1, replica_groups=mesh['parts'=1,'batch'=16,'mp'=2] {'batch'}, use_global_device_ids=true, to_apply=%add | all-reduce | flops 32 | bytes 256
  181.5 0.2 select_reduce_fusion
  181.7 0.1 iota_add_fusion
  181.8 0.1 add.45
  181.9 2.8 %fusion.3 = f32[32,2048]{1,0:T(8,128)} fusion(bf16[512,2048]{1,0:T(8,128)(2,1)} %bitcast.18, s32[512]{0:T(512)S(1)} %add.45, s32[32]{0:T(128)S(1)} %iota_add_fusion.1), kind=kOutput, calls=%fused_computation.4 | convolution fusion | flops 67125248 | bytes 2361472 | tf_op jit(solution)/shard_map/dot_general | solution.py:13
  184.7 1.2 fusion.1
  185.9 1.0 copy.30
  (10 shorter events, 0.0 us)
Async XLA Ops:
  0.6 2.5 %copy-start.2 = (bf16[2048,4]{0,1:T(4,128)(2,1)S(1)}, bf16[2048,4]{0,1:T(4,128)(2,1)}, u32[]{:S(2)}) copy-start(bf16[2048,4]{0,1:T(4,128)(2,1)} %param.11) | copy-start | bytes 49156
  3.2 1.6 copy-start
  3.2 1.6 copy-start.1
  164.6 4.1 %copy-start.5 = (u32[32]{0:T(128)S(1)}, u32[32]{0:T(128)}, u32[]{:S(2)}) copy-start(u32[32]{0:T(128)} %constant.44) | copy-start | bytes 388
  164.6 5.3 %copy-start.3 = (s32[2,1]{0,1:T(1,128)S(1)}, s32[2,1]{0,1:T(1,128)}, u32[]{:S(2)}) copy-start(s32[2,1]{0,1:T(1,128)} %param.14) | copy-start | bytes 28
  164.6 16.9 %copy-start.4 = (s32[32]{0:T(128)S(1)}, s32[32]{0:T(128)}, u32[]{:S(2)}) copy-start(s32[32]{0:T(128)} %param.15) | copy-start | bytes 388

commit v2 on v1

--- a/solution.py
+++ b/solution.py
@@ -92,10 +92,10 @@
 
 
 def fused_kernel(
-    spots, act, grad, weight, down_own, up_own,
-    out, terms,
-    wbuf, fac, gfull, acc, share, theirs,
-    w_recv, w_send, f_recv, f_send, t_recv, t_send, x_recv, x_send,
+    spots, act, grad, levels, scales_t, down_own, up_own, tag_own,
+    out, down_grads, up_grads,
+    weight, terms, tags, wbuf, fac, gfull, acc, share, theirs,
+    w_recv, w_send, f_recv, f_send, g_recv, g_send, t_recv, t_send, x_recv, x_send,
 ):
     slots, pieces, piece_rows, width = wbuf.shape
     tiles = spots.shape[0]
@@ -146,28 +146,34 @@
         else:
             pl.when(when)(moved.start)
 
-    def spread(src, dst, send, recv, k, across):
+    def along(src, dst, send, recv, k):
         from_z = near(k)
         push(src, dst, send, recv, UP, jnp.logical_and(from_z <= z, not_top))
         push(src, dst, send, recv, DOWN, jnp.logical_and(from_z >= z, not_bottom))
-        if across:
-            push(src, dst, send, recv, ACROSS)
-        push(src, dst, send, recv, SIBLING)
 
     def landed(ref, recv):
         copy(ref, ref, x_send.at[0], recv, partner).wait_recv()
 
-    def weight_on(k, plane):
+    def z_first(ref, own, send, recv, k, plane):
+        if k or plane:
+            landed(ref, recv)
+        src = own if k == 0 and plane == 0 else ref
+        if plane == 0:
+            along(src, ref, send, recv, k)
+            push(src, ref, send, recv, ACROSS)
+        push(src, ref, send, recv, SIBLING)
+
+    def y_first(ref, send, recv, k, plane):
+        if k or plane:
+            landed(ref, recv)
+        if k == 0 and plane == 0:
+            push(ref, ref, send, recv, ACROSS)
+        along(ref, ref, send, recv, k)
+        push(ref, ref, send, recv, SIBLING)
+
+    def weight_on(k, plane, p):
         s = slot(k, plane, 0)
-        for p in range(pieces):
-            dst = wbuf.at[s, p]
-            src = weight.at[p] if k == 0 and plane == 0 else dst
-            if src is dst:
-                landed(dst, w_recv.at[s, p])
-            if plane == 0:
-                spread(src, dst, w_send.at[k, p], w_recv.at[s, p], k, True)
-            else:
-                push(src, dst, w_send.at[DEPTH + k, p], w_recv.at[s, p], SIBLING)
+        z_first(wbuf.at[s, p], weight.at[p], w_send.at[plane * DEPTH + k, p], w_recv.at[s, p], k, plane)
 
     def weight_in(k, plane):
         s = slot(k, plane, 1)
@@ -189,39 +195,53 @@
 
     def factor_on(k, plane):
         s = slot(k, plane, 0)
-        if k or plane:
-            landed(fac.at[s], f_recv.at[s])
-        spread(fac.at[s], fac.at[s], f_send.at[plane * DEPTH + k], f_recv.at[s], k, k == 0 and plane == 0)
+        z_first(fac.at[s], fac.at[s], f_send.at[plane * DEPTH + k], f_recv.at[s], k, plane)
+        z_first(tags.at[s], tags.at[s], g_send.at[plane * DEPTH + k], g_recv.at[s], k, plane)
 
     def terms_on(k, plane):
         s = slot(k, plane, 0)
-        if k or plane:
-            landed(terms.at[s], t_recv.at[s])
-        if plane == 0:
-            spread(terms.at[s], terms.at[s], t_send.at[k], t_recv.at[s], k, True)
-        else:
-            push(terms.at[s], terms.at[s], t_send.at[DEPTH + k], t_recv.at[s], SIBLING)
+        y_first(terms.at[s], t_send.at[plane * DEPTH + k], t_recv.at[s], k, plane)
 
     rank = down_own.shape[1]
     for sub in range(down_own.shape[0]):
         fac[me, 0, sub] = down_own[sub]
         fac[me, 1, sub] = up_own[sub]
+    tags[me] = tag_own[...]
     factor_on(0, 0)
-    weight_on(0, 0)
     cross = copy(grad, gfull.at[half], x_send.at[0], x_recv.at[0], partner)
     cross.start()
+
+    groups = scales_t.shape[0]
+    spread = (
+        lax.broadcasted_iota(jnp.int32, (groups, width), 0)
+        == lax.broadcasted_iota(jnp.int32, (groups, width), 1) // QB
+    ).astype(jnp.bfloat16)
+
+    @pl.loop(0, pieces * piece_rows // CHUNK)
+    def _(j):
+        rows = pl.ds(pl.multiple_of(j * CHUNK, CHUNK), CHUNK)
+        inside = pl.ds(pl.multiple_of((j * CHUNK) % piece_rows, CHUNK), CHUNK)
+        factor = contract(scales_t[:, rows], spread, 0, 0)
+        weight[j * CHUNK // piece_rows, inside, :] = (
+            levels[rows, :].astype(jnp.float32) * factor
+        ).astype(jnp.bfloat16)
+
     gfull[half] = grad[...]
     share[...] = jnp.zeros_like(share)
-
-    factor_on(0, 1)
-    for k in range(1, DEPTH):
-        factor_on(k, 0)
+    factor_on(1, 0)
+    factor_on(2, 0)
+    weight_on(0, 0, 0)
+    factor_on(3, 0)
+    weight_on(0, 0, 1)
+    weight_on(1, 0, 0)
+    weight_on(1, 0, 1)
+    for k in range(DEPTH):
         factor_on(k, 1)
-    weight_on(1, 0)
     for k in range(DEPTH):
         for plane in range(2):
             s = slot(k, plane, 1)
             landed(fac.at[s], f_recv.at[s])
+            landed(tags.at[s], g_recv.at[s])
 
     tile_rows = act.shape[0] // tiles
     for t in range(tiles):
@@ -231,7 +251,7 @@
         share[1, rows, :rank] = contract(grad[rows, :], fac[where, 1, sub], 1, 1)
     swap = copy(share, theirs, x_send.at[1], x_recv.at[1], partner)
     swap.start()
-    weight_on(2, 0)
+    weight_on(2, 0, 0)
     landed(theirs, x_recv.at[1])
     for t in range(tiles):
         rows = pl.ds(t * tile_rows, tile_rows)
@@ -248,50 +268,65 @@
         turned = jnp.transpose(hidden)[:rank].astype(jnp.bfloat16)
         terms[me, 1, t] = (2.0 * contract(turned, grad[rows, :], 1, 0)).astype(jnp.bfloat16)
     terms_on(0, 0)
-
+    weight_on(2, 0, 1)
     landed(gfull.at[1 - half], x_recv.at[0])
     multiply(0, 0, 0)
+    weight_on(3, 0, 0)
     multiply(1, 0, 0)
+    weight_on(3, 0, 1)
+    terms_on(0, 1)
+    terms_on(1, 0)
+    terms_on(1, 1)
+    weight_on(0, 1, 0)
+    weight_on(0, 1, 1)
+    terms_on(2, 0)
     multiply(2, 0, 0)
-    weight_on(0, 1)
-    weight_on(1, 1)
-    weight_on(3, 0)
-    terms_on(1, 0)
+    terms_on(2, 1)
+    weight_on(1, 1, 0)
+    weight_on(1, 1, 1)
     multiply(3, 0, 0)
     weight_in(0, 0)
     multiply(0, 0, 1)
     multiply(0, 1, 0)
-    multiply(1, 1, 0)
     weight_in(1, 0)
     multiply(1, 0, 1)
-    weight_on(2, 1)
-    terms_on(2, 0)
-    multiply(2, 1, 0)
+    multiply(1, 1, 0)
+    weight_on(2, 1, 0)
+    weight_on(2, 1, 1)
+    terms_on(3, 0)
     weight_in(0, 1)
     multiply(0, 1, 1)
+    weight_in(2, 0)
+    multiply(2, 0, 1)
     weight_in(1, 1)
     multiply(1, 1, 1)
-    weight_in(2, 0)
-    multiply(2, 0, 1)
-    terms_on(3, 0)
-    terms_on(0, 1)
-    terms_on(1, 1)
+    multiply(2, 1, 0)
+    weight_on(3, 1, 0)
+    terms_on(3, 1)
     weight_in(3, 0)
     multiply(3, 0, 1)
     weight_in(2, 1)
     multiply(2, 1, 1)
-    weight_on(3, 1)
-    terms_on(2, 1)
+    weight_on(3, 1, 1)
     multiply(3, 1, 0)
-    terms_on(3, 1)
+    for k in range(DEPTH):
+        for plane in range(2):
+            s = slot(k, plane, 1)
+            landed(terms.at[s], t_recv.at[s])
+    kept, width_all = down_grads.shape[0], tags.shape[2]
+    marks = tags[0]
+    for s in range(1, slots):
+        marks = marks + tags[s]
+    own_rows = lax.broadcasted_iota(jnp.int32, (kept, width_all), 0) + (me * kept + 1)
+    pick = (own_rows == marks[:1]).astype(jnp.bfloat16)
+    for kind, grads in ((0, down_grads), (1, up_grads)):
+        for c in range(0, grads.shape[1], 512):
+            flat = terms[:, kind, :, :, c : c + 512].reshape(width_all, 512)
+            grads[:, c : c + 512] = contract(pick, flat, 1, 0)
     weight_in(3, 1)
     multiply(3, 1, 1)
     for j in range(acc.shape[0]):
         out[:, j * CHUNK : (j + 1) * CHUNK] = acc[j].astype(jnp.bfloat16)
-    for k in range(DEPTH):
-        for plane in range(2):
-            s = slot(k, plane, 1)
-            landed(terms.at[s], t_recv.at[s])
     cross.wait_send()
     swap.wait_send()
     for moved, when in started:
@@ -324,22 +359,32 @@
 
     mine = owners(tenant_per_tile[:, 0])
     spots = jnp.stack([mine // held, mine % held], axis=1)
-    everyone = lax.all_gather(tenant_per_tile, "batch", axis=0, tiled=True)
-    weight = dequantize(levels, scales).reshape(PIECES, in_rows // PIECES, out_cols)
+    terms_here = tiles_here * ADAPTER_RANK
+    row_of = jnp.repeat(mine, ADAPTER_RANK) * ADAPTER_RANK + jnp.tile(
+        jnp.arange(ADAPTER_RANK, dtype=jnp.int32), tiles_here
+    )
+    is_mine = jnp.arange(slots, dtype=jnp.int32)[:, None] == lax.axis_index("batch")
+    tag = jnp.where(is_mine, row_of[None, :] + 1, 0).reshape(1, slots * terms_here)
+    tag = jnp.broadcast_to(tag, (8, slots * terms_here))
+    weight_shape = (PIECES, in_rows // PIECES, out_cols)
     factor_shape = (held, ADAPTER_RANK, inner_local)
     vmem = pl.BlockSpec(memory_space=pltpu.VMEM)
     dma = pltpu.SemaphoreType.DMA
     bf16, f32 = jnp.bfloat16, jnp.float32
-    out, terms = pl.pallas_call(
+    return pl.pallas_call(
         fused_kernel,
         out_shape=(
             jax.ShapeDtypeStruct((rows_dev, in_rows), bf16),
-            jax.ShapeDtypeStruct((slots, 2, tiles_here, ADAPTER_RANK, inner_local), bf16),
+            jax.ShapeDtypeStruct((held * ADAPTER_RANK, inner_local), f32),
+            jax.ShapeDtypeStruct((held * ADAPTER_RANK, inner_local), f32),
         ),
-        in_specs=[pl.BlockSpec(memory_space=pltpu.SMEM)] + [vmem] * 5,
-        out_specs=(vmem, vmem),
+        in_specs=[pl.BlockSpec(memory_space=pltpu.SMEM)] + [vmem] * 7,
+        out_specs=(vmem, vmem, vmem),
         scratch_shapes=[
-            pltpu.VMEM((slots,) + weight.shape, bf16),
+            pltpu.VMEM(weight_shape, bf16),
+            pltpu.VMEM((slots, 2, tiles_here, ADAPTER_RANK, inner_local), bf16),
+            pltpu.VMEM((slots,) + tag.shape, jnp.int32),
+            pltpu.VMEM((slots,) + weight_shape, bf16),
             pltpu.VMEM((slots, 2) + factor_shape, bf16),
             pltpu.VMEM((2, rows_dev, inner_local), bf16),
             pltpu.VMEM((in_rows // CHUNK, rows_dev, CHUNK), f32),
@@ -347,6 +392,8 @@
             pltpu.VMEM((2, rows_dev, 128), f32),
             dma((slots, PIECES)),
             dma((2 * DEPTH, PIECES, 4)),
+            dma((slots,)),
+            dma((2 * DEPTH, 4)),
             dma((slots,)),
             dma((2 * DEPTH, 4)),
             dma((slots,)),
@@ -366,19 +413,12 @@
         spots,
         activations,
         output_gradient,
-        weight,
+        levels,
+        scales.T,
         adapter_down_rows.reshape(factor_shape),
         adapter_up_rows.reshape(factor_shape),
-    )
-    row_of = jnp.repeat(owners(everyone[:, 0]), ADAPTER_RANK) * ADAPTER_RANK + jnp.tile(
-        jnp.arange(ADAPTER_RANK, dtype=jnp.int32), everyone.shape[0]
-    )
-    first = lax.axis_index("batch") * held * ADAPTER_RANK
-    own_rows = first + jnp.arange(held * ADAPTER_RANK, dtype=jnp.int32)
-    pick = (own_rows[:, None] == row_of[None, :]).astype(bf16)
-    down_grads = contract(pick, terms[:, 0].reshape(-1, inner_local), 1, 0)
-    up_grads = contract(pick, terms[:, 1].reshape(-1, inner_local), 1, 0)
-    return out, down_grads, up_grads
+        tag,
+    )
 
 
 def solution(mesh):

time: 187 us -> 154 us (0.82)
  Pallas kernels: 160 us -> 146 us
  blocking collectives: 11.6 us -> 0 us
  matrix products: 3.99 us -> 0 us
  local copies, waits for them, and re-layouts: 8.68 us -> 5.74 us
    pallas_call x1, Pallas kernels: 160 us -> 146 us  [fused_body(): pl.pallas_call(fused_kernel, out_shape=(jax.ShapeDtypeStruct((rows_dev, i...]
    unnamed x1 -> x0, blocking collectives: 11.6 us -> none
    slice x1 -> x0, local copies, waits for them, and re-layouts: 4.02 us -> none  [fused_body(): up_grads = contract(pick, terms[:, 1].reshape(-1, inner_local), 1, 0)]
    dot_general x2 -> x0, matrix products: 3.99 us -> none  [contract(): lax.dot_general(left, right, (((left_dim,), (right_dim,)), ((), ())), pre...]
    unnamed x17 -> x13, local copies, waits for them, and re-layouts: 3.18 us -> 5.48 us
where the time goes in v2:
time: 154 us; the launch traced here: 153 us
  Pallas kernels  146 us (95%)
  local copies, waits for them, and re-layouts  5.74 us (4%)
    pallas_call x1, Pallas kernels, fused_body(): pl.pallas_call(fused_kernel, out_shape=(jax.ShapeDtypeStruct((rows_dev, i...  146 us
    unnamed x13, local copies, waits for them, and re-layouts  5.48 us

profile of v2, /device:TPU:0, one launch (start us, length us, event | category | flops | bytes accessed | tf_op | source)
XLA Modules:
  0.0 152.6 jit_solution(14685845856444893630)
XLA Ops:
  0.6 0.0 copy-start.3
  0.7 0.0 copy-start.4
  0.7 0.6 copy-done.3
  1.3 0.0 copy-done.4
  1.3 0.2 fusion
  1.5 0.1 add_add_fusion
  1.6 0.1 add.47
  1.7 0.1 copy.15
  1.8 0.1 pad_add_fusion.spots
  1.9 0.1 broadcast_select_fusion
  1.9 0.0 copy-start.2
  1.9 0.1 select_n.40
  2.0 0.6 copy-done.2
  2.6 0.0 copy-start
  2.6 0.9 copy-done
  3.6 0.0 copy-start.1
  3.6 0.9 copy-done.1
  4.5 145.8 %shard_map.103 = (bf16[256,2048]{1,0:T(8,128)(2,1)S(1)}, f32[32,2048]{1,0:T(8,128)S(1)}, f32[32,2048]{1,0:T(8,128)S(1)}) custom-call(s32[2,2]{1,0:T(2,128)S(1)} %pad_add_fusion.spots, bf16[256,2048]{1,0:T(8,128)(2,1)} %act.1, bf16[256,2048]{1,0:T(8,128)(2,1)} %grad.1, bf16[2048,256]{1,0:T(8,128)(2,1)} %levels.1, bf16[4,2048]{1,0:T(4,128)(2,1)S(1)} %bitcast.7, ...), custom_call_target="tpu_custom_call" | custom-call | flops 4294967296 | bytes 134217728 | tf_op jit(solution)/shard_map/pallas_call | solution.py:374
  150.2 1.0 copy.22
  151.2 0.7 copy.23
  151.9 0.7 copy.24
  (4 shorter events, 0.0 us)
Async XLA Ops:
  0.6 0.7 copy-start.3
  0.7 0.7 copy-start.4
  1.9 0.7 copy-start.2
  2.6 0.9 copy-start
  3.6 0.9 copy-start.1

commit v3 on v2

--- a/solution.py
+++ b/solution.py
@@ -187,7 +187,7 @@
         own = k == 0 and plane == 0 and column == 0
         per_piece = piece_rows // CHUNK
 
-        @pl.loop(0, pieces * per_piece)
+        @pl.loop(0, pieces * per_piece, unroll=8)
         def _(j):
             rows = pl.ds(pl.multiple_of((j % per_piece) * CHUNK, CHUNK), CHUNK)
             block = weight[j // per_piece, rows, :] if own else wbuf[s, j // per_piece, rows, :]

time: 154 us -> 142 us (0.922)
  Pallas kernels: 146 us -> 135 us
    pallas_call x1, Pallas kernels: 146 us -> 135 us  [fused_body(): pl.pallas_call(fused_kernel, out_shape=(jax.ShapeDtypeStruct((rows_dev, i...]
where the time goes in v3:
time: 142 us
  Pallas kernels  135 us (95%)
  local copies, waits for them, and re-layouts  5.74 us (4%)
    pallas_call x1, Pallas kernels, fused_body(): pl.pallas_call(fused_kernel, out_shape=(jax.ShapeDtypeStruct((rows_dev, i...  135 us
    unnamed x13, local copies, waits for them, and re-layouts  5.48 us

profile of v3, /device:TPU:0, one launch (start us, length us, event | category | flops | bytes accessed | tf_op | source)
XLA Modules:
  0.0 141.9 jit_solution(2059638143638504023)
XLA Ops:
  0.6 0.0 copy-start.3
  0.7 0.0 copy-start.4
  0.7 0.6 copy-done.3
  1.3 0.0 copy-done.4
  1.3 0.2 fusion
  1.5 0.1 add_add_fusion
  1.6 0.1 add.47
  1.7 0.1 copy.15
  1.8 0.1 pad_add_fusion.spots
  1.9 0.1 broadcast_select_fusion
  1.9 0.0 copy-start.2
  1.9 0.1 select_n.40
  2.0 0.6 copy-done.2
  2.6 0.0 copy-start
  2.6 0.9 copy-done
  3.6 0.0 copy-start.1
  3.6 0.9 copy-done.1
  4.5 135.0 %shard_map.103 = (bf16[256,2048]{1,0:T(8,128)(2,1)S(1)}, f32[32,2048]{1,0:T(8,128)S(1)}, f32[32,2048]{1,0:T(8,128)S(1)}) custom-call(s32[2,2]{1,0:T(2,128)S(1)} %pad_add_fusion.spots, bf16[256,2048]{1,0:T(8,128)(2,1)} %act.1, bf16[256,2048]{1,0:T(8,128)(2,1)} %grad.1, bf16[2048,256]{1,0:T(8,128)(2,1)} %levels.1, bf16[4,2048]{1,0:T(4,128)(2,1)S(1)} %bitcast.7, ...), custom_call_target="tpu_custom_call" | custom-call | flops 4294967296 | bytes 134217728 | tf_op jit(solution)/shard_map/pallas_call | solution.py:374
  139.5 1.0 copy.22
  140.5 0.7 copy.23
  141.2 0.7 copy.24
  (4 shorter events, 0.0 us)
Async XLA Ops:
  0.6 0.7 copy-start.3
  0.7 0.7 copy-start.4
  1.9 0.7 copy-start.2
  2.6 0.9 copy-start
  3.6 0.9 copy-start.1
